TPU v7x, 256 devices: a whole 4x4x8 slice. The times are simulated.
256 devices in a mesh: dom: 128 (over x, z, y), fn: 2 (over core).
Axes of the slice: x: 4, y: 4, z: 8, core: 2. Of those that a mesh axis runs over, the one named last changes fastest.
Arguments:
- rhs: float32 [6144, 16, 320], P('dom', 'fn'), may hold values from -6 to 6
- dinv: bfloat16 [6144, 320, 320], P('dom')
- extract: float32 [6, 320, 80], replicated, may hold values from -0.3125 to 0.3125
- lift: float32 [6, 80, 320], replicated, may hold values from -0.625 to 0.625
- coef: float32 [6144, 6], P('dom'), may hold values from 0.1 to 0.45
- nbr: int32 [6144, 6], P('dom'), may hold values from -1 to 63, as said below
- colour: int32 [6144], P('dom'), may hold values from 0 to 1
- counts: int32 [128], P('dom'), may hold values from 1 to 48, as said below
- send_lo: int32 [1024], P('dom'), may hold values from 0 to 47, as said below
- send_hi: int32 [1024], P('dom'), may hold values from 0 to 47, as said below
- rec_elem: int32 [16384], P('dom'), may hold values from 0 to 47, as said below
- rec_owner: int32 [16384, 1], P('dom'), may hold values from 0 to 127; in each aligned block of 128 rows (0 to 127, 128 to 255, ...) at most 2 rows name the same one
- rec_box: int32 [16384], P('dom'), may hold values from 0 to 3
- rec_weight: float32 [16384], P('dom'), may hold values from 0.3 to 3
- wall_map: bfloat16 [320, 128], replicated, may hold values from -0.3125 to 0.3125
- fweights: float32 [16], P('fn'), may hold values from -1.5 to 1.5
Outputs:
- grad: float32 [512, 16, 128], P('dom', 'fn')
- combined: float32 [512, 128], P('dom')
Inputs may be any that keep to these rules, and one draw needn't show every extreme that they name: `counts`: each count is at least 1, and some partition is full (48) in every draw. `nbr`: codes of a live element: -1 a wall, below 48 a live element of the same partition, 48 + s import slot s below (face 0 only), 56 + s import slot s above (face 1 only). `send_lo`: live elements of the sending partition. `send_hi`: live elements of the sending partition. `rec_elem`: live elements of the record's partition. `rec_owner`: the records of one partition name one owner at most 2 times.
All inputs are finite; a program needn't handle non-finite values.
Results may differ from a plain program's by a relative error of at most 0.0034.
Values sent between devices are 32-bit elements; how exact they have to be, the bound alone decides.
A program may use at most 64 MiB of HBM per device.

v0:
```python
import functools
import jax
import jax.numpy as jnp
from jax import lax
from jax.experimental import pallas as pl
from jax.experimental.pallas import tpu as pltpu
from jax.sharding import PartitionSpec as P

BOX_DEV = 4
SWEEPS = 2
OPPOSITE = (1, 0, 3, 2, 5, 4)
LANES = 128
GRIDS = {128: (4, 8, 4), 8: (2, 2, 2)}
MESH = pl.DeviceIdType.MESH
F32 = jnp.float32
BF16 = jnp.bfloat16


def split(value):
    high = value.astype(BF16)
    return high, (value - high.astype(F32)).astype(BF16)


def mm(a, b):
    return jnp.dot(a, b, preferred_element_type=F32)


def mm3(a_high, a_low, b_high, b_low):
    return mm(a_high, b_high) + mm(a_low, b_high) + mm(a_high, b_low)


def kernel(
    dims,
    rhs_any,
    dinv_any,
    extract_any,
    lift_any,
    coef,
    nbr,
    colour,
    counts,
    send_lo,
    send_hi,
    rec_elem,
    rec_owner,
    rec_box,
    rec_weight,
    wall_map,
    fweights,
    grad,
    combined,
    rhs,
    dinv,
    extract,
    lift,
    ext_high,
    ext_low,
    lift_high,
    lift_low,
    psi,
    table,
    near_high,
    near_low,
    resid,
    sensed,
    out_up,
    out_down,
    in_below,
    in_above,
    tab_f,
    tab_i,
    sm_f,
    sm_i,
    tabs_in,
    boxes_i,
    sm_boxes,
    send_rec,
    recv_rec,
    z_send,
    z_recv,
    part,
    part_in,
    load_sem,
    dinv_sem,
    sm_sem,
    up_sem,
    down_sem,
    tab_sem,
    rec_sem,
    z_sem,
    fn_sem,
):
    X, Z, Y = dims
    XY = X * Y
    slots, funcs, width = rhs.shape
    rows = slots * funcs
    trace = extract.shape[1]
    rim = out_up.shape[1]
    records = rec_elem.shape[1]
    owners = X * Z * Y
    chunk = slots // dinv_sem.shape[0]
    me = lax.axis_index("dom")
    fn = lax.axis_index("fn")
    x = me // (Z * Y)
    z = (me // Y) % Z
    y = me % Y
    above = lax.rem(me + 1, owners)
    below = lax.rem(me + owners - 1, owners)

    def place(px, pz, py):
        return (px * Z + pz) * Y + py

    def plane_peer(rd):
        dx, dy = rd // Y, rd % Y
        return place(lax.rem(x + dx, X), z, lax.rem(y + dy, Y))

    def back(rd):
        dx, dy = rd // Y, rd % Y
        return ((X - dx) % X) * Y + (Y - dy) % Y

    half = Z // 2
    shifts = [half]
    for step in range(1, half):
        shifts += [half - step, half + step]
    shifts += [0]

    def column(j):
        return lax.rem(z + shifts[j], Z)

    small = []
    for i, (src, dst) in enumerate(
        ((rhs_any, rhs), (extract_any, extract), (lift_any, lift))
    ):
        copy = pltpu.make_async_copy(src, dst, load_sem.at[i])
        copy.start()
        small.append(copy)
    blocks = []
    for i in range(slots // chunk):
        span = pl.ds(i * chunk, chunk)
        copy = pltpu.make_async_copy(dinv_any.at[span], dinv.at[span], dinv_sem.at[i])
        copy.start()
        blocks.append(copy)

    barrier = pltpu.get_barrier_semaphore()
    partners = [(above, fn), (below, fn), (me, 1 - fn)]
    partners += [(plane_peer(rd), fn) for rd in range(1, XY)]
    partners += [(place(x, column(j), y), fn) for j in range(Z - 1)]
    for partner in partners:
        pl.semaphore_signal(barrier, inc=1, device_id=partner, device_id_type=MESH)

    lane = lax.broadcasted_iota(jnp.int32, (records, records), 1)
    sub = lax.broadcasted_iota(jnp.int32, (records, records), 0)
    own = jnp.broadcast_to(rec_owner[...], (records, records)).astype(F32)
    own_col = jnp.sum(jnp.where(lane == sub, own, 0.0), axis=1, keepdims=True)
    same = (own == own_col) & (lane < sub)
    rank = jnp.sum(jnp.where(same, 1.0, 0.0), axis=1, keepdims=True)
    lane_o = lax.broadcasted_iota(jnp.int32, (records, owners), 1).astype(F32)
    first = jnp.where((own_col == lane_o) & (rank < 0.5), 1.0, 0.0)
    second = jnp.where((own_col == lane_o) & (rank > 0.5), 1.0, 0.0)
    row = lax.broadcasted_iota(jnp.int32, (8, records), 0)
    elem_b = jnp.broadcast_to(rec_elem[...].astype(F32), (8, records))
    box_b = jnp.broadcast_to(rec_box[...].astype(F32), (8, records))
    weight_b = jnp.broadcast_to(rec_weight[...], (8, records))

    def rows_at(s):
        return jnp.where(
            row == s, box_b, jnp.where(row == 2 + s, elem_b, jnp.where(row == 4 + s, weight_b, 0.0))
        )

    tab = jnp.dot(
        rows_at(0), first, precision=lax.Precision.HIGHEST, preferred_element_type=F32
    ) + jnp.dot(
        rows_at(1), second, precision=lax.Precision.HIGHEST, preferred_element_type=F32
    )
    tab_f[...] = tab
    tab_i[...] = jnp.clip((tab + 0.25).astype(jnp.int32), 0, slots - 1)
    to_smem = [
        pltpu.make_async_copy(tab_f, sm_f, sm_sem.at[0]),
        pltpu.make_async_copy(tab_i, sm_i, sm_sem.at[1]),
    ]
    for copy in to_smem:
        copy.start()

    table[:, 0] = jnp.zeros((6, funcs, LANES), F32)
    small[1].wait()
    small[2].wait()
    for f in range(6):
        pad = jnp.zeros((LANES - trace, width), F32)
        value = jnp.concatenate([extract[OPPOSITE[f]], pad], axis=0)
        high, low = split(value.T)
        ext_high[:, f * LANES : (f + 1) * LANES] = high
        ext_low[:, f * LANES : (f + 1) * LANES] = low
        high, low = split(lift[f])
        pad = jnp.zeros((LANES - trace, width), BF16)
        lift_high[f * LANES : (f + 1) * LANES] = jnp.concatenate([high, pad], axis=0)
        lift_low[f * LANES : (f + 1) * LANES] = jnp.concatenate([low, pad], axis=0)

    pl.semaphore_wait(barrier, len(partners))
    tab_copies = []
    for rd in range(1, XY):
        copy = pltpu.make_async_remote_copy(
            src_ref=tab_f,
            dst_ref=tabs_in.at[back(rd)],
            send_sem=tab_sem.at[0, rd],
            recv_sem=tab_sem.at[1, back(rd)],
            device_id=(plane_peer(rd), fn),
            device_id_type=MESH,
        )
        copy.start()
        tab_copies.append(copy)

    live = counts[0]

    def update(e, shade, source, first_step):
        at = pl.ds(pl.multiple_of(e * funcs, funcs), funcs)
        value = source(e).astype(BF16)
        fresh = mm(value, dinv[e])
        mask = jnp.where((colour[e] == shade) & (e < live), 1, 0)
        old = jnp.zeros((funcs, width), F32) if first_step else psi[at]
        psi[at] = jnp.where(jnp.full((funcs, width), mask, jnp.int32) > 0, fresh, old)

    small[0].wait()
    for i, copy in enumerate(blocks):
        copy.wait()
        for k in range(chunk):
            update(i * chunk + k, 0, lambda e: rhs[e], True)

    exchanges = []
    for step in range(1, 2 * SWEEPS):
        shade = step % 2
        high, low = split(psi[...])

        def fill(pair):
            cols = pl.ds(pair * 2 * LANES, 2 * LANES)
            out = mm3(high, low, ext_high[:, cols], ext_low[:, cols])
            for half_ in range(2):
                table[pair * 2 + half_, 1 : slots + 1] = out[
                    :, half_ * LANES : (half_ + 1) * LANES
                ].reshape(slots, funcs, LANES)

        fill(0)
        for s in range(rim):
            out_up[step - 1, s] = table[0, send_hi[s] + 1]
            out_down[step - 1, s] = table[1, send_lo[s] + 1]
        up = pltpu.make_async_remote_copy(
            src_ref=out_up.at[step - 1],
            dst_ref=in_below.at[step - 1],
            send_sem=up_sem.at[0, step - 1],
            recv_sem=up_sem.at[1, step - 1],
            device_id=(above, fn),
            device_id_type=MESH,
        )
        up.start()
        down = pltpu.make_async_remote_copy(
            src_ref=out_down.at[step - 1],
            dst_ref=in_above.at[step - 1],
            send_sem=down_sem.at[0, step - 1],
            recv_sem=down_sem.at[1, step - 1],
            device_id=(below, fn),
            device_id_type=MESH,
        )
        down.start()
        exchanges += [up, down]
        fill(1)
        fill(2)

        def gather(faces):
            def pairs(i, _):
                for k in range(4):
                    e = i * 8 + k * 2
                    at = pl.ds(pl.multiple_of(e * funcs, 2 * funcs), 2 * funcs)
                    for f in faces:
                        value = jnp.concatenate(
                            [
                                table[f, nbr[f, e] + 1] * coef[f, e],
                                table[f, nbr[f, e + 1] + 1] * coef[f, e + 1],
                            ],
                            axis=0,
                        )
                        h, l = split(value)
                        near_high[at, f * LANES : (f + 1) * LANES] = h
                        near_low[at, f * LANES : (f + 1) * LANES] = l
                return 0

            lax.fori_loop(0, slots // 8, pairs, 0)

        def lifted(lo, hi):
            a, b = lo * LANES, hi * LANES
            return mm3(
                near_high[:, a:b], near_low[:, a:b], lift_high[a:b], lift_low[a:b]
            )

        gather((2, 3, 4, 5))
        resid[...] = rhs[...].reshape(rows, width) - lifted(2, 6)
        up.wait_recv()
        down.wait_recv()
        table[0, slots + 1 : slots + 1 + rim] = in_below[step - 1]
        table[1, slots + 1 + rim : slots + 1 + 2 * rim] = in_above[step - 1]
        gather((0, 1))
        resid[...] = resid[...] - lifted(0, 2)

        def source(e):
            return resid[pl.ds(pl.multiple_of(e * funcs, funcs), funcs)]

        def sweep(i, _):
            for k in range(8):
                update(i * 8 + k, shade, source, False)
            return 0

        lax.fori_loop(0, slots // 8, sweep, 0)

    high, low = split(psi[...])
    sensed[...] = (mm(high, wall_map[...]) + mm(low, wall_map[...])).reshape(
        slots, funcs, LANES
    )
    for copy in to_smem:
        copy.wait()
    for copy in tab_copies:
        copy.wait_recv()
    boxes_i[0] = tab_i[...]
    boxes_i[1:] = (tabs_in[1:] + 0.25).astype(jnp.int32)
    boxes = pltpu.make_async_copy(boxes_i, sm_boxes, sm_sem.at[2])
    boxes.start()
    per = rec_sem.shape[1]
    group = Z // per
    rec_copies = []
    for c in range(per):

        def build(rd, _):
            px, py = lax.rem(x + rd // Y, X), lax.rem(y + rd % Y, Y)
            for j in range(c * group, (c + 1) * group):
                owner = place(px, column(j), py)
                for s in range(2):
                    send_rec[rd, j, s] = sensed[sm_i[2 + s, owner]] * sm_f[4 + s, owner]
            return 0

        lax.fori_loop(0, XY, build, 0)
        span = pl.ds(c * group, group)
        sent = []
        for rd in range(1, XY):
            copy = pltpu.make_async_remote_copy(
                src_ref=send_rec.at[rd, span],
                dst_ref=recv_rec.at[back(rd), span],
                send_sem=rec_sem.at[0, c, rd],
                recv_sem=rec_sem.at[1, c, back(rd)],
                device_id=(plane_peer(rd), fn),
                device_id_type=MESH,
            )
            copy.start()
            sent.append(copy)
        rec_copies.append(sent)
    boxes.wait()

    z_copies = []
    for c in range(per):
        for copy in rec_copies[c]:
            copy.wait_recv()
        for j in range(c * group, (c + 1) * group):
            owner = place(x, column(j), y)

            def add(value, box, total):
                which = jnp.full((funcs, LANES), box, jnp.int32)
                return tuple(t + jnp.where(which == b, value, 0.0) for b, t in enumerate(total))

            total = (jnp.zeros((funcs, LANES), F32),) * BOX_DEV
            for s in range(2):
                total = add(send_rec[0, j, s], sm_boxes[0, s, owner], total)

            def accumulate(rd, total):
                for s in range(2):
                    total = add(recv_rec[rd, j, s], sm_boxes[rd, s, owner], total)
                return total

            total = lax.fori_loop(1, XY, accumulate, total)
            for b in range(BOX_DEV):
                z_send[j, b] = total[b]
            if j < Z - 1:
                far = shifts.index((Z - shifts[j]) % Z)
                copy = pltpu.make_async_remote_copy(
                    src_ref=z_send.at[j],
                    dst_ref=z_recv.at[far],
                    send_sem=z_sem.at[0, j],
                    recv_sem=z_sem.at[1, far],
                    device_id=(place(x, column(j), y), fn),
                    device_id_type=MESH,
                )
                copy.start()
                z_copies.append(copy)

    result = z_send[Z - 1]
    for copy in z_copies:
        copy.wait_recv()
    for j in range(Z - 1):
        result = result + z_recv[j]
    grad[...] = result

    sub_f = lax.broadcasted_iota(jnp.int32, (funcs, LANES), 0)
    scale = jnp.zeros((funcs, LANES), F32)
    for j in range(funcs):
        scale = jnp.where(sub_f == j, fweights[j], scale)
    part[...] = jnp.sum(result * scale[None], axis=1)
    pair = pltpu.make_async_remote_copy(
        src_ref=part,
        dst_ref=part_in,
        send_sem=fn_sem.at[0],
        recv_sem=fn_sem.at[1],
        device_id=(me, 1 - fn),
        device_id_type=MESH,
    )
    pair.start()
    pair.wait_recv()
    combined[...] = part[...] + part_in[...]

    pair.wait_send()
    for copy in tab_copies + exchanges + z_copies:
        copy.wait_send()
    for sent in rec_copies:
        for copy in sent:
            copy.wait_send()


def body(
    rhs,
    dinv,
    extract,
    lift,
    coef,
    nbr,
    colour,
    counts,
    send_lo,
    send_hi,
    rec_elem,
    rec_owner,
    rec_box,
    rec_weight,
    wall_map,
    fweights,
):
    slots, funcs, width = rhs.shape
    rim = send_lo.shape[0]
    records = rec_elem.shape[0]
    owners = lax.axis_size("dom")
    X, Z, Y = GRIDS[owners]
    rows = slots * funcs
    steps = 2 * SWEEPS - 1
    blocks = 8
    per = min(4, Z)
    any_ = pl.BlockSpec(memory_space=pl.ANY)
    smem = pl.BlockSpec(memory_space=pltpu.SMEM)
    vmem = pl.BlockSpec(memory_space=pltpu.VMEM)
    dma = pltpu.SemaphoreType.DMA
    return pl.pallas_call(
        functools.partial(kernel, (X, Z, Y)),
        out_shape=(
            jax.ShapeDtypeStruct((BOX_DEV, funcs, LANES), F32),
            jax.ShapeDtypeStruct((BOX_DEV, LANES), F32),
        ),
        in_specs=[any_] * 4 + [smem] * 6 + [vmem] * 5 + [smem],
        out_specs=(vmem, vmem),
        scratch_shapes=[
            pltpu.VMEM(rhs.shape, F32),
            pltpu.VMEM(dinv.shape, BF16),
            pltpu.VMEM(lift.shape, F32),
            pltpu.VMEM(lift.shape, F32),
            pltpu.VMEM((width, 6 * LANES), BF16),
            pltpu.VMEM((width, 6 * LANES), BF16),
            pltpu.VMEM((6 * LANES, width), BF16),
            pltpu.VMEM((6 * LANES, width), BF16),
            pltpu.VMEM((rows, width), F32),
            pltpu.VMEM((6, slots + 2 * rim + 1, funcs, LANES), F32),
            pltpu.VMEM((rows, 6 * LANES), BF16),
            pltpu.VMEM((rows, 6 * LANES), BF16),
            pltpu.VMEM((rows, width), F32),
            pltpu.VMEM((slots, funcs, LANES), F32),
            pltpu.VMEM((steps, rim, funcs, LANES), F32),
            pltpu.VMEM((steps, rim, funcs, LANES), F32),
            pltpu.VMEM((steps, rim, funcs, LANES), F32),
            pltpu.VMEM((steps, rim, funcs, LANES), F32),
            pltpu.VMEM((8, owners), F32),
            pltpu.VMEM((8, owners), jnp.int32),
            pltpu.SMEM((8, owners), F32),
            pltpu.SMEM((8, owners), jnp.int32),
            pltpu.VMEM((X * Y, 8, owners), F32),
            pltpu.VMEM((X * Y, 8, owners), jnp.int32),
            pltpu.SMEM((X * Y, 8, owners), jnp.int32),
            pltpu.VMEM((X * Y, Z, 2, funcs, LANES), F32),
            pltpu.VMEM((X * Y, Z, 2, funcs, LANES), F32),
            pltpu.VMEM((Z, BOX_DEV, funcs, LANES), F32),
            pltpu.VMEM((Z, BOX_DEV, funcs, LANES), F32),
            pltpu.VMEM((BOX_DEV, LANES), F32),
            pltpu.VMEM((BOX_DEV, LANES), F32),
            dma((3,)),
            dma((blocks,)),
            dma((3,)),
            dma((2, steps)),
            dma((2, steps)),
            dma((2, X * Y)),
            dma((2, per, X * Y)),
            dma((2, Z)),
            dma((2,)),
        ],
        compiler_params=pltpu.CompilerParams(
            collective_id=0, has_side_effects=True, vmem_limit_bytes=48 * 1024 * 1024
        ),
    )(
        rhs,
        dinv,
        extract.transpose(0, 2, 1),
        lift,
        coef.T,
        nbr.T,
        colour,
        counts,
        send_lo,
        send_hi,
        rec_elem.reshape(1, records),
        rec_owner.T,
        rec_box.reshape(1, records),
        rec_weight.reshape(1, records),
        wall_map,
        fweights,
    )


def solution(mesh):
    placed = (
        P("dom", "fn", None),
        P("dom", None, None),
        P(),
        P(),
        P("dom", None),
        P("dom", None),
        P("dom"),
        P("dom"),
        P("dom"),
        P("dom"),
        P("dom"),
        P("dom", None),
        P("dom"),
        P("dom"),
        P(),
        P("fn"),
    )
    return jax.shard_map(
        body,
        mesh=mesh,
        in_specs=placed,
        out_specs=(P("dom", "fn", None), P("dom", None)),
        check_vma=False,
    )
```

profile of v0, /device:TPU:1, one launch (start us, length us, event | category | flops | bytes accessed | tf_op | source)
XLA Modules:
  0.0 75.6 jit_solution(8142348194427179263)
XLA Ops:
  1.3 0.0 copy-start
  1.3 1.1 %copy-done = f32[6,320,80]{1,2,0:T(8,128)S(1)} copy-done((f32[6,320,80]{1,2,0:T(8,128)S(1)}, f32[6,320,80]{1,2,0:T(8,128)}, u32[]{:S(2)}) %copy-start) | copy-done | bytes 614424
  2.4 0.0 copy-start.1
  2.4 1.1 %copy-done.1 = f32[6,80,320]{2,1,0:T(8,128)S(1)} copy-done((f32[6,80,320]{2,1,0:T(8,128)S(1)}, f32[6,80,320]{2,1,0:T(8,128)}, u32[]{:S(2)}) %copy-start.1) | copy-done | bytes 614424
  3.5 0.0 copy-start.2
  3.5 1.1 %copy-done.2 = f32[48,8,320]{2,1,0:T(8,128)S(1)} copy-done((f32[48,8,320]{2,1,0:T(8,128)S(1)}, f32[48,8,320]{2,1,0:T(8,128)}, u32[]{:S(2)}) %copy-start.2) | copy-done | bytes 491544
  4.6 0.0 copy-start.3
  4.6 0.9 %copy-done.3 = bf16[320,128]{1,0:T(8,128)(2,1)S(1)} copy-done((bf16[320,128]{1,0:T(8,128)(2,1)S(1)}, bf16[320,128]{1,0:T(8,128)(2,1)}, u32[]{:S(2)}) %copy-start.3) | copy-done | bytes 81944
  5.5 0.0 copy-start.4
  5.5 0.7 copy-done.4
  6.2 0.0 copy-start.5
  6.2 0.7 copy-done.5
  6.8 0.0 copy-start.6
  6.8 0.7 copy-done.6
  7.5 0.0 copy-start.7
  7.5 0.7 copy-done.7
  8.2 0.0 copy-start.8
  8.2 0.7 copy-done.8
  8.8 0.0 copy-start.9
  8.8 0.7 copy-done.9
  9.5 0.0 copy-start.10
  9.5 0.7 copy-done.10
  10.1 0.0 copy-start.11
  10.1 0.7 copy-done.11
  10.8 0.0 copy-start.12
  10.8 0.7 copy-done.12
  11.4 0.0 copy-start.13
  11.4 0.7 copy-done.13
  12.1 62.3 %shard_map.167 = (f32[4,8,128]{2,1,0:T(8,128)S(1)}, f32[4,128]{1,0:T(4,128)S(1)}) custom-call(f32[48,8,320]{2,1,0:T(8,128)S(1)} %copy-done.2, bf16[48,320,320]{2,1,0:T(8,128)(2,1)} %dinv_any.1, f32[6,80,320]{2,1,0:T(8,128)S(1)} %bitcast.7, f32[6,80,320]{2,1,0:T(8,128)S(1)} %copy-done.1, f32[6,48]{1,0:T(8,128)S(1)} %bitcast.8, s32[6,48]{1,0:T(8,128)S(1)} %bitcast.9, ...), custom_call_target="tpu_custom_call" | custom-call | tf_op jit(solution)/shard_map/pallas_call | solution.py:453
  74.4 0.6 copy.21
  75.0 0.6 copy.22
Async XLA Ops:
  1.3 1.1 %copy-start = (f32[6,320,80]{1,2,0:T(8,128)S(1)}, f32[6,320,80]{1,2,0:T(8,128)}, u32[]{:S(2)}) copy-start(f32[6,320,80]{1,2,0:T(8,128)} %param.18) | copy-start | bytes 1843204
  2.4 1.1 %copy-start.1 = (f32[6,80,320]{2,1,0:T(8,128)S(1)}, f32[6,80,320]{2,1,0:T(8,128)}, u32[]{:S(2)}) copy-start(f32[6,80,320]{2,1,0:T(8,128)} %lift_any.1) | copy-start | bytes 1843204
  3.5 1.1 %copy-start.2 = (f32[48,8,320]{2,1,0:T(8,128)S(1)}, f32[48,8,320]{2,1,0:T(8,128)}, u32[]{:S(2)}) copy-start(f32[48,8,320]{2,1,0:T(8,128)} %rhs_any.1) | copy-start | bytes 1474564
  4.6 0.9 %copy-start.3 = (bf16[320,128]{1,0:T(8,128)(2,1)S(1)}, bf16[320,128]{1,0:T(8,128)(2,1)}, u32[]{:S(2)}) copy-start(bf16[320,128]{1,0:T(8,128)(2,1)} %wall_map.1) | copy-start | bytes 245764
  5.5 0.7 copy-start.4
  6.2 0.7 copy-start.5
  6.8 0.7 copy-start.6
  7.5 0.7 copy-start.7
  8.2 0.7 copy-start.8
  8.8 0.7 copy-start.9
  9.5 0.7 copy-start.10
  10.1 0.7 copy-start.11
  10.8 0.7 copy-start.12
  11.4 0.7 copy-start.13
where the time goes:
time: 76 us; the launch traced here: 75.6 us
  Pallas kernels  62.3 us (82%)
  local copies, waits for them, and re-layouts  12 us (16%)
  between operations  1.31 us (2%)
    pallas_call x1, Pallas kernels, body(): pl.pallas_call(functools.partial(kernel, (X, Z, Y)), out_shape=(jax.Shape...  62.3 us
    unnamed x30, local copies, waits for them, and re-layouts  12 us

commit v1 on v0

--- a/solution.py
+++ b/solution.py
@@ -25,16 +25,30 @@
     return jnp.dot(a, b, preferred_element_type=F32)
 
 
-def mm3(a_high, a_low, b_high, b_low):
-    return mm(a_high, b_high) + mm(a_low, b_high) + mm(a_high, b_low)
-
-
 def kernel(
     dims,
-    rhs_any,
-    dinv_any,
-    extract_any,
-    lift_any,
+    rhs_hbm,
+    dinv_hbm,
+    extract_hbm,
+    lift_hbm,
+    coef_hbm,
+    nbr_hbm,
+    colour_hbm,
+    counts_hbm,
+    send_lo_hbm,
+    send_hi_hbm,
+    rec_elem_hbm,
+    rec_owner_hbm,
+    rec_box_hbm,
+    rec_weight_hbm,
+    wall_map_hbm,
+    fweights_hbm,
+    grad,
+    combined,
+    rhs,
+    dinv,
+    extract,
+    lift,
     coef,
     nbr,
     colour,
@@ -47,18 +61,11 @@
     rec_weight,
     wall_map,
     fweights,
-    grad,
-    combined,
-    rhs,
-    dinv,
-    extract,
-    lift,
-    ext_high,
-    ext_low,
-    lift_high,
-    lift_low,
+    ext_cat,
+    lift_cat,
     psi,
     table,
+    scale,
     near_high,
     near_low,
     resid,
@@ -114,6 +121,9 @@
         dx, dy = rd // Y, rd % Y
         return place(lax.rem(x + dx, X), z, lax.rem(y + dy, Y))
 
+    def wait_for(ref, sem):
+        pltpu.make_async_copy(ref, ref, sem).wait()
+
     def back(rd):
         dx, dy = rd // Y, rd % Y
         return ((X - dx) % X) * Y + (Y - dy) % Y
@@ -127,17 +137,32 @@
     def column(j):
         return lax.rem(z + shifts[j], Z)
 
+    order = (
+        (rec_owner_hbm, rec_owner),
+        (rec_elem_hbm, rec_elem),
+        (rec_box_hbm, rec_box),
+        (rec_weight_hbm, rec_weight),
+        (colour_hbm, colour),
+        (counts_hbm, counts),
+        (coef_hbm, coef),
+        (nbr_hbm, nbr),
+        (send_lo_hbm, send_lo),
+        (send_hi_hbm, send_hi),
+        (rhs_hbm, rhs),
+        (extract_hbm, extract),
+        (lift_hbm, lift),
+        (wall_map_hbm, wall_map),
+        (fweights_hbm, fweights),
+    )
     small = []
-    for i, (src, dst) in enumerate(
-        ((rhs_any, rhs), (extract_any, extract), (lift_any, lift))
-    ):
+    for i, (src, dst) in enumerate(order):
         copy = pltpu.make_async_copy(src, dst, load_sem.at[i])
         copy.start()
         small.append(copy)
     blocks = []
     for i in range(slots // chunk):
         span = pl.ds(i * chunk, chunk)
-        copy = pltpu.make_async_copy(dinv_any.at[span], dinv.at[span], dinv_sem.at[i])
+        copy = pltpu.make_async_copy(dinv_hbm.at[span], dinv.at[span], dinv_sem.at[i])
         copy.start()
         blocks.append(copy)
 
@@ -145,9 +170,12 @@
     partners = [(above, fn), (below, fn), (me, 1 - fn)]
     partners += [(plane_peer(rd), fn) for rd in range(1, XY)]
     partners += [(place(x, column(j), y), fn) for j in range(Z - 1)]
+    partners += [(place(x, column(j), y), 1 - fn) for j in range(Z - 1)]
     for partner in partners:
         pl.semaphore_signal(barrier, inc=1, device_id=partner, device_id_type=MESH)
 
+    for copy in small[:4]:
+        copy.wait()
     lane = lax.broadcasted_iota(jnp.int32, (records, records), 1)
     sub = lax.broadcasted_iota(jnp.int32, (records, records), 0)
     own = jnp.broadcast_to(rec_owner[...], (records, records)).astype(F32)
@@ -181,58 +209,76 @@
     for copy in to_smem:
         copy.start()
 
+    full = width // (2 * LANES) * 2 * LANES
     table[:, 0] = jnp.zeros((6, funcs, LANES), F32)
-    small[1].wait()
-    small[2].wait()
+    small[11].wait()
+    small[12].wait()
     for f in range(6):
         pad = jnp.zeros((LANES - trace, width), F32)
         value = jnp.concatenate([extract[OPPOSITE[f]], pad], axis=0)
         high, low = split(value.T)
-        ext_high[:, f * LANES : (f + 1) * LANES] = high
-        ext_low[:, f * LANES : (f + 1) * LANES] = low
-        high, low = split(lift[f])
-        pad = jnp.zeros((LANES - trace, width), BF16)
-        lift_high[f * LANES : (f + 1) * LANES] = jnp.concatenate([high, pad], axis=0)
-        lift_low[f * LANES : (f + 1) * LANES] = jnp.concatenate([low, pad], axis=0)
-
+        cols = slice(f * LANES, (f + 1) * LANES)
+        pieces = [high[:full], high[:full], low[:full], high[full:], high[full:], low[full:]]
+        if 3 * width < ext_cat.shape[0]:
+            pieces += [jnp.zeros((ext_cat.shape[0] - 3 * width, LANES), BF16)]
+        ext_cat[:, cols] = jnp.concatenate(pieces, axis=0)
+        pad = jnp.zeros((LANES - trace, width), F32)
+        high, low = split(jnp.concatenate([lift[f], pad], axis=0))
+        lift_cat[0, f * LANES : (f + 1) * LANES] = high
+        lift_cat[1, f * LANES : (f + 1) * LANES] = low
+
+    small[6].wait()
+
+    def spread(i, _):
+        for k in range(8):
+            for f in range(6):
+                scale[f, i * 8 + k] = jnp.full((funcs, LANES), coef[f, i * 8 + k], F32)
+        return 0
+
+    lax.fori_loop(0, slots // 8, spread, 0)
+    small[4].wait()
+    small[5].wait()
+    live = counts[0]
+    batch = slots // 2
+
+    def update(first_e, count, shade, source, first_step):
+        fresh = []
+        for k in range(count):
+            value = source(first_e + k).astype(BF16)
+            fresh.append(mm(value, dinv[first_e + k]))
+        for k in range(count):
+            e = first_e + k
+            mask = jnp.where((colour[e] == shade) & (e < live), 1, 0)
+            mask = jnp.full((funcs, width), mask, jnp.int32) > 0
+            at = pl.ds(pl.multiple_of(e * funcs, funcs), funcs)
+            old = jnp.zeros((funcs, width), F32) if first_step else psi[at]
+            psi[at] = jnp.where(mask, fresh[k], old)
+
+    small[10].wait()
+
+    def start(i, _):
+        span = pl.ds(i * chunk, chunk)
+        pltpu.make_async_copy(dinv_hbm.at[span], dinv.at[span], dinv_sem.at[i]).wait()
+        update(i * chunk, chunk, 0, lambda e: rhs[e], True)
+        return 0
+
+    lax.fori_loop(0, slots // chunk, start, 0)
+
+    for i in (7, 8, 9, 13, 14):
+        small[i].wait()
     pl.semaphore_wait(barrier, len(partners))
-    tab_copies = []
-    for rd in range(1, XY):
-        copy = pltpu.make_async_remote_copy(
-            src_ref=tab_f,
-            dst_ref=tabs_in.at[back(rd)],
-            send_sem=tab_sem.at[0, rd],
-            recv_sem=tab_sem.at[1, back(rd)],
-            device_id=(plane_peer(rd), fn),
-            device_id_type=MESH,
-        )
-        copy.start()
-        tab_copies.append(copy)
-
-    live = counts[0]
-
-    def update(e, shade, source, first_step):
-        at = pl.ds(pl.multiple_of(e * funcs, funcs), funcs)
-        value = source(e).astype(BF16)
-        fresh = mm(value, dinv[e])
-        mask = jnp.where((colour[e] == shade) & (e < live), 1, 0)
-        old = jnp.zeros((funcs, width), F32) if first_step else psi[at]
-        psi[at] = jnp.where(jnp.full((funcs, width), mask, jnp.int32) > 0, fresh, old)
-
-    small[0].wait()
-    for i, copy in enumerate(blocks):
-        copy.wait()
-        for k in range(chunk):
-            update(i * chunk + k, 0, lambda e: rhs[e], True)
-
-    exchanges = []
-    for step in range(1, 2 * SWEEPS):
-        shade = step % 2
+    def step_body(step, _):
+        shade = lax.rem(step, 2)
         high, low = split(psi[...])
+        pieces = [high[:, :full], low[:, :full], high[:, :full]]
+        pieces += [high[:, full:], low[:, full:], high[:, full:]]
+        if 3 * width < ext_cat.shape[0]:
+            pieces += [jnp.zeros((rows, ext_cat.shape[0] - 3 * width), BF16)]
+        state = jnp.concatenate(pieces, axis=1)
 
         def fill(pair):
             cols = pl.ds(pair * 2 * LANES, 2 * LANES)
-            out = mm3(high, low, ext_high[:, cols], ext_low[:, cols])
+            out = mm(state, ext_cat[:, cols])
             for half_ in range(2):
                 table[pair * 2 + half_, 1 : slots + 1] = out[
                     :, half_ * LANES : (half_ + 1) * LANES
@@ -245,8 +291,8 @@
         up = pltpu.make_async_remote_copy(
             src_ref=out_up.at[step - 1],
             dst_ref=in_below.at[step - 1],
-            send_sem=up_sem.at[0, step - 1],
-            recv_sem=up_sem.at[1, step - 1],
+            send_sem=up_sem.at[0],
+            recv_sem=up_sem.at[step],
             device_id=(above, fn),
             device_id_type=MESH,
         )
@@ -254,41 +300,45 @@
         down = pltpu.make_async_remote_copy(
             src_ref=out_down.at[step - 1],
             dst_ref=in_above.at[step - 1],
-            send_sem=down_sem.at[0, step - 1],
-            recv_sem=down_sem.at[1, step - 1],
+            send_sem=down_sem.at[0],
+            recv_sem=down_sem.at[step],
             device_id=(below, fn),
             device_id_type=MESH,
         )
         down.start()
-        exchanges += [up, down]
         fill(1)
         fill(2)
 
         def gather(faces):
             def pairs(i, _):
-                for k in range(4):
-                    e = i * 8 + k * 2
-                    at = pl.ds(pl.multiple_of(e * funcs, 2 * funcs), 2 * funcs)
-                    for f in faces:
-                        value = jnp.concatenate(
-                            [
-                                table[f, nbr[f, e] + 1] * coef[f, e],
-                                table[f, nbr[f, e + 1] + 1] * coef[f, e + 1],
-                            ],
-                            axis=0,
+                for f in faces:
+                    found = []
+                    for k in range(4):
+                        e = i * 8 + k * 2
+                        found.append(
+                            jnp.concatenate(
+                                [
+                                    table[f, nbr[f, e] + 1] * scale[f, e],
+                                    table[f, nbr[f, e + 1] + 1] * scale[f, e + 1],
+                                ],
+                                axis=0,
+                            )
                         )
-                        h, l = split(value)
-                        near_high[at, f * LANES : (f + 1) * LANES] = h
-                        near_low[at, f * LANES : (f + 1) * LANES] = l
+                    found = [split(value) for value in found]
+                    for k in range(4):
+                        start = pl.multiple_of((i * 8 + k * 2) * funcs, 2 * funcs)
+                        at = pl.ds(start, 2 * funcs)
+                        near_high[at, f * LANES : (f + 1) * LANES] = found[k][0]
+                        near_low[at, f * LANES : (f + 1) * LANES] = found[k][1]
                 return 0
 
             lax.fori_loop(0, slots // 8, pairs, 0)
 
         def lifted(lo, hi):
             a, b = lo * LANES, hi * LANES
-            return mm3(
-                near_high[:, a:b], near_low[:, a:b], lift_high[a:b], lift_low[a:b]
-            )
+            left = jnp.concatenate([near_high[:, a:b], near_low[:, a:b], near_high[:, a:b]], axis=1)
+            right = jnp.concatenate([lift_cat[0, a:b], lift_cat[0, a:b], lift_cat[1, a:b]], axis=0)
+            return mm(left, right)
 
         gather((2, 3, 4, 5))
         resid[...] = rhs[...].reshape(rows, width) - lifted(2, 6)
@@ -303,27 +353,39 @@
             return resid[pl.ds(pl.multiple_of(e * funcs, funcs), funcs)]
 
         def sweep(i, _):
-            for k in range(8):
-                update(i * 8 + k, shade, source, False)
+            update(i * batch, batch, shade, source, False)
             return 0
 
-        lax.fori_loop(0, slots // 8, sweep, 0)
-
+        lax.fori_loop(0, slots // batch, sweep, 0)
+        up.wait_send()
+        down.wait_send()
+        return 0
+
+    lax.fori_loop(1, 2 * SWEEPS, step_body, 0)
+
+    for rd in range(1, XY):
+        copy = pltpu.make_async_remote_copy(
+            src_ref=tab_f,
+            dst_ref=tabs_in.at[back(rd)],
+            send_sem=tab_sem.at[0],
+            recv_sem=tab_sem.at[1],
+            device_id=(plane_peer(rd), fn),
+            device_id_type=MESH,
+        )
+        copy.start()
     high, low = split(psi[...])
     sensed[...] = (mm(high, wall_map[...]) + mm(low, wall_map[...])).reshape(
         slots, funcs, LANES
     )
     for copy in to_smem:
         copy.wait()
-    for copy in tab_copies:
-        copy.wait_recv()
+    wait_for(tabs_in.at[1:], tab_sem.at[1])
     boxes_i[0] = tab_i[...]
     boxes_i[1:] = (tabs_in[1:] + 0.25).astype(jnp.int32)
     boxes = pltpu.make_async_copy(boxes_i, sm_boxes, sm_sem.at[2])
     boxes.start()
-    per = rec_sem.shape[1]
+    per = rec_sem.shape[0] - 1
     group = Z // per
-    rec_copies = []
     for c in range(per):
 
         def build(rd, _):
@@ -336,25 +398,24 @@
 
         lax.fori_loop(0, XY, build, 0)
         span = pl.ds(c * group, group)
-        sent = []
         for rd in range(1, XY):
             copy = pltpu.make_async_remote_copy(
                 src_ref=send_rec.at[rd, span],
                 dst_ref=recv_rec.at[back(rd), span],
-                send_sem=rec_sem.at[0, c, rd],
-                recv_sem=rec_sem.at[1, c, back(rd)],
+                send_sem=rec_sem.at[per],
+                recv_sem=rec_sem.at[c],
                 device_id=(plane_peer(rd), fn),
                 device_id_type=MESH,
             )
             copy.start()
-            sent.append(copy)
-        rec_copies.append(sent)
     boxes.wait()
 
-    z_copies = []
+    sub_f = lax.broadcasted_iota(jnp.int32, (funcs, LANES), 0)
+    weight = jnp.zeros((funcs, LANES), F32)
+    for j in range(funcs):
+        weight = jnp.where(sub_f == j, fweights[j], weight)
     for c in range(per):
-        for copy in rec_copies[c]:
-            copy.wait_recv()
+        wait_for(recv_rec.at[1:, pl.ds(c * group, group)], rec_sem.at[c])
         for j in range(c * group, (c + 1) * group):
             owner = place(x, column(j), y)
 
@@ -374,49 +435,46 @@
             total = lax.fori_loop(1, XY, accumulate, total)
             for b in range(BOX_DEV):
                 z_send[j, b] = total[b]
+            far = shifts.index((Z - shifts[j]) % Z)
+            part[j] = jnp.concatenate(
+                [jnp.sum(total[b] * weight, axis=0, keepdims=True) for b in range(BOX_DEV)], axis=0
+            )
+            copy = pltpu.make_async_remote_copy(
+                src_ref=part.at[j],
+                dst_ref=part_in.at[far],
+                send_sem=fn_sem.at[0],
+                recv_sem=fn_sem.at[1],
+                device_id=(place(x, column(j), y), 1 - fn),
+                device_id_type=MESH,
+            )
+            copy.start()
             if j < Z - 1:
-                far = shifts.index((Z - shifts[j]) % Z)
                 copy = pltpu.make_async_remote_copy(
                     src_ref=z_send.at[j],
                     dst_ref=z_recv.at[far],
-                    send_sem=z_sem.at[0, j],
-                    recv_sem=z_sem.at[1, far],
+                    send_sem=z_sem.at[0],
+                    recv_sem=z_sem.at[1],
                     device_id=(place(x, column(j), y), fn),
                     device_id_type=MESH,
                 )
                 copy.start()
-                z_copies.append(copy)
 
     result = z_send[Z - 1]
-    for copy in z_copies:
-        copy.wait_recv()
+    wait_for(z_recv.at[: Z - 1], z_sem.at[1])
+    wait_for(part_in, fn_sem.at[1])
     for j in range(Z - 1):
         result = result + z_recv[j]
     grad[...] = result
 
-    sub_f = lax.broadcasted_iota(jnp.int32, (funcs, LANES), 0)
-    scale = jnp.zeros((funcs, LANES), F32)
-    for j in range(funcs):
-        scale = jnp.where(sub_f == j, fweights[j], scale)
-    part[...] = jnp.sum(result * scale[None], axis=1)
-    pair = pltpu.make_async_remote_copy(
-        src_ref=part,
-        dst_ref=part_in,
-        send_sem=fn_sem.at[0],
-        recv_sem=fn_sem.at[1],
-        device_id=(me, 1 - fn),
-        device_id_type=MESH,
-    )
-    pair.start()
-    pair.wait_recv()
-    combined[...] = part[...] + part_in[...]
-
-    pair.wait_send()
-    for copy in tab_copies + exchanges + z_copies:
-        copy.wait_send()
-    for sent in rec_copies:
-        for copy in sent:
-            copy.wait_send()
+    own_part = jnp.sum(result * weight[None], axis=1)
+    for j in range(Z):
+        own_part = own_part + part_in[j]
+    combined[...] = own_part
+
+    wait_for(tabs_in.at[1:], tab_sem.at[0])
+    wait_for(send_rec.at[1:], rec_sem.at[per])
+    wait_for(z_send.at[: Z - 1], z_sem.at[0])
+    wait_for(part, fn_sem.at[0])
 
 
 def body(
@@ -446,8 +504,7 @@
     steps = 2 * SWEEPS - 1
     blocks = 8
     per = min(4, Z)
-    any_ = pl.BlockSpec(memory_space=pl.ANY)
-    smem = pl.BlockSpec(memory_space=pltpu.SMEM)
+    hbm = pl.BlockSpec(memory_space=pltpu.HBM)
     vmem = pl.BlockSpec(memory_space=pltpu.VMEM)
     dma = pltpu.SemaphoreType.DMA
     return pl.pallas_call(
@@ -456,19 +513,30 @@
             jax.ShapeDtypeStruct((BOX_DEV, funcs, LANES), F32),
             jax.ShapeDtypeStruct((BOX_DEV, LANES), F32),
         ),
-        in_specs=[any_] * 4 + [smem] * 6 + [vmem] * 5 + [smem],
+        in_specs=[hbm] * 16,
         out_specs=(vmem, vmem),
         scratch_shapes=[
             pltpu.VMEM(rhs.shape, F32),
             pltpu.VMEM(dinv.shape, BF16),
             pltpu.VMEM(lift.shape, F32),
             pltpu.VMEM(lift.shape, F32),
-            pltpu.VMEM((width, 6 * LANES), BF16),
-            pltpu.VMEM((width, 6 * LANES), BF16),
-            pltpu.VMEM((6 * LANES, width), BF16),
-            pltpu.VMEM((6 * LANES, width), BF16),
+            pltpu.SMEM((6, slots), F32),
+            pltpu.SMEM((6, slots), jnp.int32),
+            pltpu.SMEM((slots,), jnp.int32),
+            pltpu.SMEM((1,), jnp.int32),
+            pltpu.SMEM((rim,), jnp.int32),
+            pltpu.SMEM((rim,), jnp.int32),
+            pltpu.VMEM((1, records), jnp.int32),
+            pltpu.VMEM((1, records), jnp.int32),
+            pltpu.VMEM((1, records), jnp.int32),
+            pltpu.VMEM((1, records), F32),
+            pltpu.VMEM(wall_map.shape, BF16),
+            pltpu.SMEM((funcs,), F32),
+            pltpu.VMEM((pl.cdiv(3 * width, 2 * LANES) * 2 * LANES, 6 * LANES), BF16),
+            pltpu.VMEM((2, 6 * LANES, width), BF16),
             pltpu.VMEM((rows, width), F32),
             pltpu.VMEM((6, slots + 2 * rim + 1, funcs, LANES), F32),
+            pltpu.VMEM((6, slots, funcs, LANES), F32),
             pltpu.VMEM((rows, 6 * LANES), BF16),
             pltpu.VMEM((rows, 6 * LANES), BF16),
             pltpu.VMEM((rows, width), F32),
@@ -488,20 +556,20 @@
             pltpu.VMEM((X * Y, Z, 2, funcs, LANES), F32),
             pltpu.VMEM((Z, BOX_DEV, funcs, LANES), F32),
             pltpu.VMEM((Z, BOX_DEV, funcs, LANES), F32),
-            pltpu.VMEM((BOX_DEV, LANES), F32),
-            pltpu.VMEM((BOX_DEV, LANES), F32),
-            dma((3,)),
+            pltpu.VMEM((Z, BOX_DEV, LANES), F32),
+            pltpu.VMEM((Z, BOX_DEV, LANES), F32),
+            dma((15,)),
             dma((blocks,)),
             dma((3,)),
-            dma((2, steps)),
-            dma((2, steps)),
-            dma((2, X * Y)),
-            dma((2, per, X * Y)),
-            dma((2, Z)),
+            dma((1 + steps,)),
+            dma((1 + steps,)),
+            dma((2,)),
+            dma((per + 1,)),
+            dma((2,)),
             dma((2,)),
         ],
         compiler_params=pltpu.CompilerParams(
-            collective_id=0, has_side_effects=True, vmem_limit_bytes=48 * 1024 * 1024
+            collective_id=0, has_side_effects=True, vmem_limit_bytes=64 * 1024 * 1024
         ),
     )(
         rhs,

time: 76 us -> 65.4 us (0.86)
  local copies, waits for them, and re-layouts: 12 us -> 2.55 us
  Pallas kernels: 62.3 us -> 61.3 us
    unnamed x30 -> x2, local copies, waits for them, and re-layouts: 12 us -> 2.55 us
    pallas_call x1, Pallas kernels: 62.3 us -> 61.3 us  [body(): pl.pallas_call(functools.partial(kernel, (X, Z, Y)), out_shape=(jax.Shape...]
where the time goes in v1:
time: 65.4 us; the launch traced here: 65.1 us
  Pallas kernels  61.3 us (94%)
  local copies, waits for them, and re-layouts  2.55 us (4%)
  between operations  1.29 us (2%)
    pallas_call x1, Pallas kernels, body(): pl.pallas_call(functools.partial(kernel, (X, Z, Y)), out_shape=(jax.Shape...  61.3 us
    unnamed x2, local copies, waits for them, and re-layouts  2.55 us

profile of v1, /device:TPU:1, one launch (start us, length us, event | category | flops | bytes accessed | tf_op | source)
XLA Modules:
  0.0 65.1 jit_solution(11858575122941410707)
XLA Ops:
  1.3 61.3 %shard_map.167 = (f32[4,8,128]{2,1,0:T(8,128)}, f32[4,128]{1,0:T(4,128)}) custom-call(f32[48,8,320]{2,1,0:T(8,128)} %rhs_hbm.1, bf16[48,320,320]{2,1,0:T(8,128)(2,1)} %dinv_hbm.1, f32[6,80,320]{2,1,0:T(8,128)} %bitcast.7, f32[6,80,320]{2,1,0:T(8,128)} %lift_hbm.1, f32[6,48]{1,0:T(8,128)} %bitcast.8, s32[6,48]{1,0:T(8,128)} %bitcast.9, s32[48]{0:T(128)} %colour_hbm.1, ...), custom_call_target="tpu_custom_call" | custom-call | tf_op jit(solution)/shard_map/pallas_call | solution.py:510
  62.6 1.3 %copy.21 = f32[4,8,128]{2,1,0:T(8,128)} copy(f32[4,8,128]{2,1,0:T(8,128)} %get-tuple-element.4) | data formatting | bytes 32768
  63.9 1.2 %copy.22 = f32[4,128]{1,0:T(4,128)} copy(f32[4,128]{1,0:T(4,128)} %get-tuple-element.5) | data formatting | bytes 4096

commit v2 on v1

--- a/solution.py
+++ b/solution.py
@@ -23,6 +23,26 @@
 
 def mm(a, b):
     return jnp.dot(a, b, preferred_element_type=F32)
+
+
+def far_displacements(X, Y):
+    def hops(rd):
+        dx, dy = rd // Y, rd % Y
+        return min(dx, X - dx) + min(dy, Y - dy)
+
+    longest = 3 if X == 4 else 2
+    return [rd for rd in range(X * Y) if hops(rd) == longest]
+
+
+def hand_over(grad_in, combined_in, grad, combined, sem):
+    copies = [
+        pltpu.make_async_copy(grad_in, grad, sem.at[0]),
+        pltpu.make_async_copy(combined_in, combined, sem.at[1]),
+    ]
+    for copy in copies:
+        copy.start()
+    for copy in copies:
+        copy.wait()
 
 
 def kernel(
@@ -87,6 +107,12 @@
     z_recv,
     part,
     part_in,
+    far_send,
+    far_recv,
+    last_send,
+    last_recv,
+    last_part,
+    last_part_in,
     load_sem,
     dinv_sem,
     sm_sem,
@@ -95,7 +121,8 @@
     tab_sem,
     rec_sem,
     z_sem,
-    fn_sem,
+    far_sem,
+    last_sem,
 ):
     X, Z, Y = dims
     XY = X * Y
@@ -128,6 +155,10 @@
         dx, dy = rd // Y, rd % Y
         return ((X - dx) % X) * Y + (Y - dy) % Y
 
+    far_first = far_displacements(X, Y)
+    near_first = [rd for rd in range(XY) if rd not in far_first]
+    A, B = len(near_first), len(far_first)
+
     half = Z // 2
     shifts = [half]
     for step in range(1, half):
@@ -136,6 +167,9 @@
 
     def column(j):
         return lax.rem(z + shifts[j], Z)
+
+    def opposite(j):
+        return shifts.index((Z - shifts[j]) % Z)
 
     order = (
         (rec_owner_hbm, rec_owner),
@@ -169,6 +203,7 @@
     barrier = pltpu.get_barrier_semaphore()
     partners = [(above, fn), (below, fn), (me, 1 - fn)]
     partners += [(plane_peer(rd), fn) for rd in range(1, XY)]
+    partners += [(plane_peer(rd), 1 - fn) for rd in far_first]
     partners += [(place(x, column(j), y), fn) for j in range(Z - 1)]
     partners += [(place(x, column(j), y), 1 - fn) for j in range(Z - 1)]
     for partner in partners:
@@ -306,6 +341,23 @@
             device_id_type=MESH,
         )
         down.start()
+
+        @pl.when(step == 1)
+        def _():
+            homes = [
+                (plane_peer(rd), near_first.index(back(rd))) for rd in near_first[1:]
+            ]
+            homes += [(place(x, column(j), y), A + opposite(j)) for j in range(Z - 1)]
+            for peer, home in homes:
+                pltpu.make_async_remote_copy(
+                    src_ref=tab_f,
+                    dst_ref=tabs_in.at[home],
+                    send_sem=tab_sem.at[0],
+                    recv_sem=tab_sem.at[1],
+                    device_id=(peer, fn),
+                    device_id_type=MESH,
+                ).start()
+
         fill(1)
         fill(2)
 
@@ -363,118 +415,173 @@
 
     lax.fori_loop(1, 2 * SWEEPS, step_body, 0)
 
-    for rd in range(1, XY):
-        copy = pltpu.make_async_remote_copy(
-            src_ref=tab_f,
-            dst_ref=tabs_in.at[back(rd)],
-            send_sem=tab_sem.at[0],
-            recv_sem=tab_sem.at[1],
-            device_id=(plane_peer(rd), fn),
-            device_id_type=MESH,
-        )
-        copy.start()
     high, low = split(psi[...])
     sensed[...] = (mm(high, wall_map[...]) + mm(low, wall_map[...])).reshape(
         slots, funcs, LANES
     )
     for copy in to_smem:
         copy.wait()
-    wait_for(tabs_in.at[1:], tab_sem.at[1])
-    boxes_i[0] = tab_i[...]
-    boxes_i[1:] = (tabs_in[1:] + 0.25).astype(jnp.int32)
+
+    def slot(owner, which):
+        return sensed[sm_i[2 + which, owner]] * sm_f[4 + which, owner]
+
+    for j in range(Z):
+        for d, rd in enumerate(far_first):
+            px, py = lax.rem(x + rd // Y, X), lax.rem(y + rd % Y, Y)
+            for which in range(2):
+                far_send[j, d, which] = slot(place(px, column(j), py), which)
+        if j < Z - 1:
+            pltpu.make_async_remote_copy(
+                src_ref=far_send.at[j],
+                dst_ref=far_recv.at[opposite(j)],
+                send_sem=far_sem.at[0],
+                recv_sem=far_sem.at[1],
+                device_id=(place(x, column(j), y), fn),
+                device_id_type=MESH,
+            ).start()
+    per = rec_sem.shape[0] - 1
+    group = Z // per
+
+    def send_near(c):
+        span = pl.ds(c * group, group)
+        for a, rd in enumerate(near_first):
+            px, py = lax.rem(x + rd // Y, X), lax.rem(y + rd % Y, Y)
+            for j in range(c * group, (c + 1) * group):
+                for which in range(2):
+                    send_rec[a, j, which] = slot(place(px, column(j), py), which)
+            if a:
+                pltpu.make_async_remote_copy(
+                    src_ref=send_rec.at[a, span],
+                    dst_ref=recv_rec.at[near_first.index(back(rd)), span],
+                    send_sem=rec_sem.at[per],
+                    recv_sem=rec_sem.at[c],
+                    device_id=(plane_peer(rd), fn),
+                    device_id_type=MESH,
+                ).start()
+
+    for c in range(per):
+        send_near(c)
+    wait_for(tabs_in.at[1 : A + Z - 1], tab_sem.at[1])
+    tabs_in[0] = tab_f[...]
+    tabs_in[A + Z - 1] = tab_f[...]
+    boxes_i[...] = (tabs_in[...] + 0.25).astype(jnp.int32)
     boxes = pltpu.make_async_copy(boxes_i, sm_boxes, sm_sem.at[2])
     boxes.start()
-    per = rec_sem.shape[0] - 1
-    group = Z // per
-    for c in range(per):
-
-        def build(rd, _):
-            px, py = lax.rem(x + rd // Y, X), lax.rem(y + rd % Y, Y)
-            for j in range(c * group, (c + 1) * group):
-                owner = place(px, column(j), py)
-                for s in range(2):
-                    send_rec[rd, j, s] = sensed[sm_i[2 + s, owner]] * sm_f[4 + s, owner]
-            return 0
-
-        lax.fori_loop(0, XY, build, 0)
-        span = pl.ds(c * group, group)
-        for rd in range(1, XY):
-            copy = pltpu.make_async_remote_copy(
-                src_ref=send_rec.at[rd, span],
-                dst_ref=recv_rec.at[back(rd), span],
-                send_sem=rec_sem.at[per],
-                recv_sem=rec_sem.at[c],
-                device_id=(plane_peer(rd), fn),
-                device_id_type=MESH,
-            )
-            copy.start()
     boxes.wait()
 
     sub_f = lax.broadcasted_iota(jnp.int32, (funcs, LANES), 0)
     weight = jnp.zeros((funcs, LANES), F32)
     for j in range(funcs):
         weight = jnp.where(sub_f == j, fweights[j], weight)
-    for c in range(per):
+    none = (jnp.zeros((funcs, LANES), F32),) * BOX_DEV
+
+    def add(value, box, total):
+        which = jnp.full((funcs, LANES), box, jnp.int32)
+        return tuple(t + jnp.where(which == b, value, 0.0) for b, t in enumerate(total))
+
+    def weighted(total):
+        return jnp.concatenate(
+            [jnp.sum(total[b] * weight, axis=0, keepdims=True) for b in range(BOX_DEV)], axis=0
+        )
+
+    def hand_on(total, full, summed, at, full_in, summed_in, home, peer, sems):
+        for b in range(BOX_DEV):
+            full[at, b] = total[b]
+        summed[at] = weighted(total)
+        pltpu.make_async_remote_copy(
+            src_ref=summed.at[at],
+            dst_ref=summed_in.at[home],
+            send_sem=sems.at[2],
+            recv_sem=sems.at[3],
+            device_id=(peer, 1 - fn),
+            device_id_type=MESH,
+        ).start()
+        pltpu.make_async_remote_copy(
+            src_ref=full.at[at],
+            dst_ref=full_in.at[home],
+            send_sem=sems.at[0],
+            recv_sem=sems.at[1],
+            device_id=(peer, fn),
+            device_id_type=MESH,
+        ).start()
+
+    def near_sums(c):
         wait_for(recv_rec.at[1:, pl.ds(c * group, group)], rec_sem.at[c])
         for j in range(c * group, (c + 1) * group):
             owner = place(x, column(j), y)
-
-            def add(value, box, total):
-                which = jnp.full((funcs, LANES), box, jnp.int32)
-                return tuple(t + jnp.where(which == b, value, 0.0) for b, t in enumerate(total))
-
-            total = (jnp.zeros((funcs, LANES), F32),) * BOX_DEV
+            total = none
             for s in range(2):
                 total = add(send_rec[0, j, s], sm_boxes[0, s, owner], total)
 
-            def accumulate(rd, total):
+            def accumulate(a, total):
                 for s in range(2):
-                    total = add(recv_rec[rd, j, s], sm_boxes[rd, s, owner], total)
+                    total = add(recv_rec[a, j, s], sm_boxes[a, s, owner], total)
                 return total
 
-            total = lax.fori_loop(1, XY, accumulate, total)
-            for b in range(BOX_DEV):
-                z_send[j, b] = total[b]
-            far = shifts.index((Z - shifts[j]) % Z)
-            part[j] = jnp.concatenate(
-                [jnp.sum(total[b] * weight, axis=0, keepdims=True) for b in range(BOX_DEV)], axis=0
+            total = lax.fori_loop(1, A, accumulate, total)
+            if j < Z - 1:
+                peer = place(x, column(j), y)
+                hand_on(total, z_send, part, j, z_recv, part_in, opposite(j), peer, z_sem)
+            else:
+                for b in range(BOX_DEV):
+                    z_send[j, b] = total[b]
+                part[j] = weighted(total)
+                pltpu.make_async_remote_copy(
+                    src_ref=part.at[j],
+                    dst_ref=part_in.at[j],
+                    send_sem=z_sem.at[2],
+                    recv_sem=z_sem.at[3],
+                    device_id=(me, 1 - fn),
+                    device_id_type=MESH,
+                ).start()
+
+    def far_sums():
+        wait_for(far_recv.at[: Z - 1], far_sem.at[1])
+        for d, rd in enumerate(far_first):
+            px, py = lax.rem(x + rd // Y, X), lax.rem(y + rd % Y, Y)
+            owner = place(px, z, py)
+            total = none
+            for s in range(2):
+                total = add(far_send[Z - 1, d, s], sm_boxes[A + Z - 1, s, owner], total)
+
+            def accumulate(j, total):
+                for s in range(2):
+                    total = add(far_recv[j, d, s], sm_boxes[A + j, s, owner], total)
+                return total
+
+            total = lax.fori_loop(0, Z - 1, accumulate, total)
+            home = far_first.index(back(rd))
+            hand_on(
+                total, last_send, last_part, d, last_recv, last_part_in, home, owner, last_sem
             )
-            copy = pltpu.make_async_remote_copy(
-                src_ref=part.at[j],
-                dst_ref=part_in.at[far],
-                send_sem=fn_sem.at[0],
-                recv_sem=fn_sem.at[1],
-                device_id=(place(x, column(j), y), 1 - fn),
-                device_id_type=MESH,
-            )
-            copy.start()
-            if j < Z - 1:
-                copy = pltpu.make_async_remote_copy(
-                    src_ref=z_send.at[j],
-                    dst_ref=z_recv.at[far],
-                    send_sem=z_sem.at[0],
-                    recv_sem=z_sem.at[1],
-                    device_id=(place(x, column(j), y), fn),
-                    device_id_type=MESH,
-                )
-                copy.start()
+
+    for c in range(per):
+        near_sums(c)
+        if c == per // 2 - 1:
+            far_sums()
 
     result = z_send[Z - 1]
     wait_for(z_recv.at[: Z - 1], z_sem.at[1])
-    wait_for(part_in, fn_sem.at[1])
+    wait_for(part_in, z_sem.at[3])
+    own_part = part_in[Z - 1]
     for j in range(Z - 1):
         result = result + z_recv[j]
+        own_part = own_part + part_in[j]
+    wait_for(last_recv, last_sem.at[1])
+    wait_for(last_part_in, last_sem.at[3])
+    for d in range(B):
+        result = result + last_recv[d]
+        own_part = own_part + last_part_in[d]
     grad[...] = result
-
-    own_part = jnp.sum(result * weight[None], axis=1)
-    for j in range(Z):
-        own_part = own_part + part_in[j]
-    combined[...] = own_part
-
-    wait_for(tabs_in.at[1:], tab_sem.at[0])
+    combined[...] = own_part + jnp.sum(result * weight[None], axis=1)
+
+    wait_for(tabs_in.at[1 : A + Z - 1], tab_sem.at[0])
     wait_for(send_rec.at[1:], rec_sem.at[per])
     wait_for(z_send.at[: Z - 1], z_sem.at[0])
-    wait_for(part, fn_sem.at[0])
+    wait_for(part, z_sem.at[2])
+    wait_for(far_send.at[: Z - 1], far_sem.at[0])
+    wait_for(last_send, last_sem.at[0])
+    wait_for(last_part, last_sem.at[2])
 
 
 def body(
@@ -504,10 +611,12 @@
     steps = 2 * SWEEPS - 1
     blocks = 8
     per = min(4, Z)
+    B = len(far_displacements(X, Y))
+    A = X * Y - B
     hbm = pl.BlockSpec(memory_space=pltpu.HBM)
     vmem = pl.BlockSpec(memory_space=pltpu.VMEM)
     dma = pltpu.SemaphoreType.DMA
-    return pl.pallas_call(
+    sums = pl.pallas_call(
         functools.partial(kernel, (X, Z, Y)),
         out_shape=(
             jax.ShapeDtypeStruct((BOX_DEV, funcs, LANES), F32),
@@ -549,15 +658,21 @@
             pltpu.VMEM((8, owners), jnp.int32),
             pltpu.SMEM((8, owners), F32),
             pltpu.SMEM((8, owners), jnp.int32),
-            pltpu.VMEM((X * Y, 8, owners), F32),
-            pltpu.VMEM((X * Y, 8, owners), jnp.int32),
-            pltpu.SMEM((X * Y, 8, owners), jnp.int32),
-            pltpu.VMEM((X * Y, Z, 2, funcs, LANES), F32),
-            pltpu.VMEM((X * Y, Z, 2, funcs, LANES), F32),
+            pltpu.VMEM((A + Z, 8, owners), F32),
+            pltpu.VMEM((A + Z, 8, owners), jnp.int32),
+            pltpu.SMEM((A + Z, 8, owners), jnp.int32),
+            pltpu.VMEM((A, Z, 2, funcs, LANES), F32),
+            pltpu.VMEM((A, Z, 2, funcs, LANES), F32),
             pltpu.VMEM((Z, BOX_DEV, funcs, LANES), F32),
             pltpu.VMEM((Z, BOX_DEV, funcs, LANES), F32),
             pltpu.VMEM((Z, BOX_DEV, LANES), F32),
             pltpu.VMEM((Z, BOX_DEV, LANES), F32),
+            pltpu.VMEM((Z, B, 2, funcs, LANES), F32),
+            pltpu.VMEM((Z, B, 2, funcs, LANES), F32),
+            pltpu.VMEM((B, BOX_DEV, funcs, LANES), F32),
+            pltpu.VMEM((B, BOX_DEV, funcs, LANES), F32),
+            pltpu.VMEM((B, BOX_DEV, LANES), F32),
+            pltpu.VMEM((B, BOX_DEV, LANES), F32),
             dma((15,)),
             dma((blocks,)),
             dma((3,)),
@@ -565,8 +680,9 @@
             dma((1 + steps,)),
             dma((2,)),
             dma((per + 1,)),
+            dma((4,)),
             dma((2,)),
-            dma((2,)),
+            dma((4,)),
         ],
         compiler_params=pltpu.CompilerParams(
             collective_id=0, has_side_effects=True, vmem_limit_bytes=64 * 1024 * 1024
@@ -589,6 +705,17 @@
         wall_map,
         fweights,
     )
+    return pl.pallas_call(
+        hand_over,
+        out_shape=(
+            jax.ShapeDtypeStruct((BOX_DEV, funcs, LANES), F32),
+            jax.ShapeDtypeStruct((BOX_DEV, LANES), F32),
+        ),
+        in_specs=[hbm] * 2,
+        out_specs=(hbm, hbm),
+        scratch_shapes=[dma((2,))],
+        compiler_params=pltpu.CompilerParams(vmem_limit_bytes=64 * 1024 * 1024),
+    )(*sums)
 
 
 def solution(mesh):

time: 65.4 us -> 57.5 us (0.88); the launches traced: 65.1 us -> 56.3 us
  Pallas kernels: 61.3 us -> 55.1 us
  local copies, waits for them, and re-layouts: 2.55 us -> 0 us
    pallas_call x1, Pallas kernels: 61.3 us -> 53.4 us  [body(): pl.pallas_call(functools.partial(kernel, (X, Z, Y)), out_shape=(jax.Shape...]
    unnamed x2 -> x0, local copies, waits for them, and re-layouts: 2.55 us -> none
    pallas_call x0 -> x1, Pallas kernels: none -> 1.68 us  [body(): pl.pallas_call(hand_over, out_shape=(jax.ShapeDtypeStruct((BOX_DEV, funcs...]
where the time goes in v2:
time: 57.5 us; the launch traced here: 56.3 us
  Pallas kernels  55.1 us (96%)
  between operations  1.29 us (2%)
    pallas_call x1, Pallas kernels, body(): pl.pallas_call(functools.partial(kernel, (X, Z, Y)), out_shape=(jax.Shape...  53.4 us
    pallas_call x1, Pallas kernels, body(): pl.pallas_call(hand_over, out_shape=(jax.ShapeDtypeStruct((BOX_DEV, funcs...  1.68 us

profile of v2, /device:TPU:1, one launch (start us, length us, event | category | flops | bytes accessed | tf_op | source)
XLA Modules:
  0.0 56.3 jit_solution(9645521047468261110)
XLA Ops:
  1.3 53.4 %shard_map.167 = (f32[4,8,128]{2,1,0:T(8,128)}, f32[4,128]{1,0:T(4,128)}) custom-call(f32[48,8,320]{2,1,0:T(8,128)} %rhs_hbm.1, bf16[48,320,320]{2,1,0:T(8,128)(2,1)} %dinv_hbm.1, f32[6,80,320]{2,1,0:T(8,128)} %bitcast.7, f32[6,80,320]{2,1,0:T(8,128)} %lift_hbm.1, f32[6,48]{1,0:T(8,128)} %bitcast.8, s32[6,48]{1,0:T(8,128)} %bitcast.9, s32[48]{0:T(128)} %colour_hbm.1, ...), custom_call_target="tpu_custom_call" | custom-call | tf_op jit(solution)/shard_map/pallas_call | solution.py:619
  54.7 1.7 %shard_map.168 = (f32[4,8,128]{2,1,0:T(8,128)}, f32[4,128]{1,0:T(4,128)}) custom-call(f32[4,8,128]{2,1,0:T(8,128)} %get-tuple-element.4.grad_in, f32[4,128]{1,0:T(4,128)} %get-tuple-element.5.combined_in), custom_call_target="tpu_custom_call" | custom-call | tf_op jit(solution)/shard_map/pallas_call | solution.py:708

commit v3 on v2

--- a/solution.py
+++ b/solution.py
@@ -193,12 +193,15 @@
         copy = pltpu.make_async_copy(src, dst, load_sem.at[i])
         copy.start()
         small.append(copy)
-    blocks = []
-    for i in range(slots // chunk):
+    chunks = slots // chunk
+
+    def block(i):
         span = pl.ds(i * chunk, chunk)
-        copy = pltpu.make_async_copy(dinv_hbm.at[span], dinv.at[span], dinv_sem.at[i])
-        copy.start()
-        blocks.append(copy)
+        return pltpu.make_async_copy(dinv_hbm.at[span], dinv.at[span], dinv_sem.at[i])
+
+    ahead = 3
+    for i in range(ahead):
+        block(i).start()
 
     barrier = pltpu.get_barrier_semaphore()
     partners = [(above, fn), (below, fn), (me, 1 - fn)]
@@ -276,6 +279,10 @@
     live = counts[0]
     batch = slots // 2
 
+    def chosen(e, shade):
+        mask = jnp.where((colour[e] == shade) & (e < live), 1, 0)
+        return jnp.full((funcs, width), mask, jnp.int32) > 0
+
     def update(first_e, count, shade, source, first_step):
         fresh = []
         for k in range(count):
@@ -283,66 +290,75 @@
             fresh.append(mm(value, dinv[first_e + k]))
         for k in range(count):
             e = first_e + k
-            mask = jnp.where((colour[e] == shade) & (e < live), 1, 0)
-            mask = jnp.full((funcs, width), mask, jnp.int32) > 0
-            at = pl.ds(pl.multiple_of(e * funcs, funcs), funcs)
-            old = jnp.zeros((funcs, width), F32) if first_step else psi[at]
-            psi[at] = jnp.where(mask, fresh[k], old)
+            old = jnp.zeros((funcs, width), F32) if first_step else psi[e]
+            psi[e] = jnp.where(chosen(e, shade), fresh[k], old)
+
+    def terms(value):
+        high, low = split(value)
+        pieces = [high[:, :full], low[:, :full], high[:, :full]]
+        pieces += [high[:, full:], low[:, full:], high[:, full:]]
+        if 3 * width < ext_cat.shape[0]:
+            pieces += [jnp.zeros((value.shape[0], ext_cat.shape[0] - 3 * width), BF16)]
+        return jnp.concatenate(pieces, axis=1)
+
+    def fill(first_e, count):
+        span = pl.ds(first_e, count)
+        out = mm(terms(psi[span].reshape(count * funcs, width)), ext_cat[...])
+        for f in range(6):
+            table[f, pl.ds(first_e + 1, count)] = out[:, f * LANES : (f + 1) * LANES].reshape(
+                count, funcs, LANES
+            )
 
     small[10].wait()
 
     def start(i, _):
-        span = pl.ds(i * chunk, chunk)
-        pltpu.make_async_copy(dinv_hbm.at[span], dinv.at[span], dinv_sem.at[i]).wait()
+        block(i).wait()
+
+        @pl.when(i + ahead < chunks)
+        def _():
+            block(i + ahead).start()
+
         update(i * chunk, chunk, 0, lambda e: rhs[e], True)
         return 0
 
-    lax.fori_loop(0, slots // chunk, start, 0)
-
+    lax.fori_loop(0, chunks, start, 0)
     for i in (7, 8, 9, 13, 14):
         small[i].wait()
     pl.semaphore_wait(barrier, len(partners))
-    def step_body(step, _):
-        shade = lax.rem(step, 2)
-        high, low = split(psi[...])
-        pieces = [high[:, :full], low[:, :full], high[:, :full]]
-        pieces += [high[:, full:], low[:, full:], high[:, full:]]
-        if 3 * width < ext_cat.shape[0]:
-            pieces += [jnp.zeros((rows, ext_cat.shape[0] - 3 * width), BF16)]
-        state = jnp.concatenate(pieces, axis=1)
-
-        def fill(pair):
-            cols = pl.ds(pair * 2 * LANES, 2 * LANES)
-            out = mm(state, ext_cat[:, cols])
-            for half_ in range(2):
-                table[pair * 2 + half_, 1 : slots + 1] = out[
-                    :, half_ * LANES : (half_ + 1) * LANES
-                ].reshape(slots, funcs, LANES)
-
-        fill(0)
-        for s in range(rim):
-            out_up[step - 1, s] = table[0, send_hi[s] + 1]
-            out_down[step - 1, s] = table[1, send_lo[s] + 1]
+    def chain(index):
         up = pltpu.make_async_remote_copy(
-            src_ref=out_up.at[step - 1],
-            dst_ref=in_below.at[step - 1],
+            src_ref=out_up.at[index],
+            dst_ref=in_below.at[index],
             send_sem=up_sem.at[0],
-            recv_sem=up_sem.at[step],
+            recv_sem=up_sem.at[1 + index],
             device_id=(above, fn),
             device_id_type=MESH,
         )
-        up.start()
         down = pltpu.make_async_remote_copy(
-            src_ref=out_down.at[step - 1],
-            dst_ref=in_above.at[step - 1],
+            src_ref=out_down.at[index],
+            dst_ref=in_above.at[index],
             send_sem=down_sem.at[0],
-            recv_sem=down_sem.at[step],
+            recv_sem=down_sem.at[1 + index],
             device_id=(below, fn),
             device_id_type=MESH,
         )
-        down.start()
-
-        @pl.when(step == 1)
+        return up, down
+
+    def export(index, away):
+        out = mm(terms(jnp.concatenate(away, axis=0)), ext_cat[:, : 2 * LANES])
+        count = rim * funcs
+        out_up[index] = out[:count, :LANES].reshape(rim, funcs, LANES)
+        out_down[index] = out[count:, LANES:].reshape(rim, funcs, LANES)
+        for copy in chain(index):
+            copy.start()
+
+    listed = [send_hi[s] for s in range(rim)] + [send_lo[s] for s in range(rim)]
+    export(0, [psi[e] for e in listed])
+
+    def step_body(step, _):
+        shade = lax.rem(step, 2)
+
+        @pl.when(step == 2)
         def _():
             homes = [
                 (plane_peer(rd), near_first.index(back(rd))) for rd in near_first[1:]
@@ -358,8 +374,9 @@
                     device_id_type=MESH,
                 ).start()
 
-        fill(1)
-        fill(2)
+        @pl.when(step > 0)
+        def _():
+            fill(0, slots)
 
         def gather(faces):
             def pairs(i, _):
@@ -393,29 +410,31 @@
             return mm(left, right)
 
         gather((2, 3, 4, 5))
-        resid[...] = rhs[...].reshape(rows, width) - lifted(2, 6)
-        up.wait_recv()
-        down.wait_recv()
+        resid[...] = rhs[...] - lifted(2, 6).reshape(slots, funcs, width)
+        for copy in chain(step - 1):
+            copy.wait_recv()
         table[0, slots + 1 : slots + 1 + rim] = in_below[step - 1]
         table[1, slots + 1 + rim : slots + 1 + 2 * rim] = in_above[step - 1]
         gather((0, 1))
-        resid[...] = resid[...] - lifted(0, 2)
-
-        def source(e):
-            return resid[pl.ds(pl.multiple_of(e * funcs, funcs), funcs)]
+        resid[...] = resid[...] - lifted(0, 2).reshape(slots, funcs, width)
+
+        @pl.when(step < 2 * SWEEPS - 1)
+        def _():
+            fresh = [mm(resid[e].astype(BF16), dinv[e]) for e in listed]
+            export(
+                step, [jnp.where(chosen(e, shade), new, psi[e]) for e, new in zip(listed, fresh)]
+            )
 
         def sweep(i, _):
-            update(i * batch, batch, shade, source, False)
+            update(i * batch, batch, shade, lambda e: resid[e], False)
             return 0
 
         lax.fori_loop(0, slots // batch, sweep, 0)
-        up.wait_send()
-        down.wait_send()
         return 0
 
     lax.fori_loop(1, 2 * SWEEPS, step_body, 0)
 
-    high, low = split(psi[...])
+    high, low = split(psi[...].reshape(rows, width))
     sensed[...] = (mm(high, wall_map[...]) + mm(low, wall_map[...])).reshape(
         slots, funcs, LANES
     )
@@ -575,6 +594,8 @@
     grad[...] = result
     combined[...] = own_part + jnp.sum(result * weight[None], axis=1)
 
+    wait_for(out_up, up_sem.at[0])
+    wait_for(out_down, down_sem.at[0])
     wait_for(tabs_in.at[1 : A + Z - 1], tab_sem.at[0])
     wait_for(send_rec.at[1:], rec_sem.at[per])
     wait_for(z_send.at[: Z - 1], z_sem.at[0])
@@ -643,12 +664,12 @@
             pltpu.SMEM((funcs,), F32),
             pltpu.VMEM((pl.cdiv(3 * width, 2 * LANES) * 2 * LANES, 6 * LANES), BF16),
             pltpu.VMEM((2, 6 * LANES, width), BF16),
-            pltpu.VMEM((rows, width), F32),
+            pltpu.VMEM((slots, funcs, width), F32),
             pltpu.VMEM((6, slots + 2 * rim + 1, funcs, LANES), F32),
             pltpu.VMEM((6, slots, funcs, LANES), F32),
             pltpu.VMEM((rows, 6 * LANES), BF16),
             pltpu.VMEM((rows, 6 * LANES), BF16),
-            pltpu.VMEM((rows, width), F32),
+            pltpu.VMEM((slots, funcs, width), F32),
             pltpu.VMEM((slots, funcs, LANES), F32),
             pltpu.VMEM((steps, rim, funcs, LANES), F32),
             pltpu.VMEM((steps, rim, funcs, LANES), F32),

time: 57.5 us -> 52 us (0.904); the launches traced: 56.3 us -> 51.6 us
  Pallas kernels: 55.1 us -> 50.3 us
    pallas_call x1, Pallas kernels: 53.4 us -> 48.6 us  [body(): pl.pallas_call(functools.partial(kernel, (X, Z, Y)), out_shape=(jax.Shape...]
where the time goes in v3:
time: 52 us; the launch traced here: 51.6 us
  Pallas kernels  50.3 us (97%)
  between operations  1.29 us (2%)
    pallas_call x1, Pallas kernels, body(): pl.pallas_call(functools.partial(kernel, (X, Z, Y)), out_shape=(jax.Shape...  48.6 us
    pallas_call x1, Pallas kernels, body(): pl.pallas_call(hand_over, out_shape=(jax.ShapeDtypeStruct((BOX_DEV, funcs...  1.68 us

profile of v3, /device:TPU:1, one launch (start us, length us, event | category | flops | bytes accessed | tf_op | source)
XLA Modules:
  0.0 51.6 jit_solution(3762684730255601393)
XLA Ops:
  1.3 48.6 %shard_map.167 = (f32[4,8,128]{2,1,0:T(8,128)}, f32[4,128]{1,0:T(4,128)}) custom-call(f32[48,8,320]{2,1,0:T(8,128)} %rhs_hbm.1, bf16[48,320,320]{2,1,0:T(8,128)(2,1)} %dinv_hbm.1, f32[6,80,320]{2,1,0:T(8,128)} %bitcast.7, f32[6,80,320]{2,1,0:T(8,128)} %lift_hbm.1, f32[6,48]{1,0:T(8,128)} %bitcast.8, s32[6,48]{1,0:T(8,128)} %bitcast.9, s32[48]{0:T(128)} %colour_hbm.1, ...), custom_call_target="tpu_custom_call" | custom-call | tf_op jit(solution)/shard_map/pallas_call | solution.py:640
  49.9 1.7 %shard_map.168 = (f32[4,8,128]{2,1,0:T(8,128)}, f32[4,128]{1,0:T(4,128)}) custom-call(f32[4,8,128]{2,1,0:T(8,128)} %get-tuple-element.4.grad_in, f32[4,128]{1,0:T(4,128)} %get-tuple-element.5.combined_in), custom_call_target="tpu_custom_call" | custom-call | tf_op jit(solution)/shard_map/pallas_call | solution.py:729

commit v4 on v3

--- a/solution.py
+++ b/solution.py
@@ -144,9 +144,11 @@
     def place(px, pz, py):
         return (px * Z + pz) * Y + py
 
+    across = [lax.rem(x + dx, X) for dx in range(X)]
+    along = [lax.rem(y + dy, Y) for dy in range(Y)]
+
     def plane_peer(rd):
-        dx, dy = rd // Y, rd % Y
-        return place(lax.rem(x + dx, X), z, lax.rem(y + dy, Y))
+        return place(across[rd // Y], z, along[rd % Y])
 
     def wait_for(ref, sem):
         pltpu.make_async_copy(ref, ref, sem).wait()
@@ -165,8 +167,10 @@
         shifts += [half - step, half + step]
     shifts += [0]
 
+    columns = [lax.rem(z + shift, Z) for shift in shifts]
+
     def column(j):
-        return lax.rem(z + shifts[j], Z)
+        return columns[j]
 
     def opposite(j):
         return shifts.index((Z - shifts[j]) % Z)
@@ -277,7 +281,7 @@
     small[4].wait()
     small[5].wait()
     live = counts[0]
-    batch = slots // 2
+    batch = slots
 
     def chosen(e, shade):
         mask = jnp.where((colour[e] == shade) & (e < live), 1, 0)
@@ -446,9 +450,10 @@
 
     for j in range(Z):
         for d, rd in enumerate(far_first):
-            px, py = lax.rem(x + rd // Y, X), lax.rem(y + rd % Y, Y)
+            px, py = across[rd // Y], along[rd % Y]
             for which in range(2):
                 far_send[j, d, which] = slot(place(px, column(j), py), which)
+    for j in range(Z):
         if j < Z - 1:
             pltpu.make_async_remote_copy(
                 src_ref=far_send.at[j],
@@ -464,10 +469,11 @@
     def send_near(c):
         span = pl.ds(c * group, group)
         for a, rd in enumerate(near_first):
-            px, py = lax.rem(x + rd // Y, X), lax.rem(y + rd % Y, Y)
+            px, py = across[rd // Y], along[rd % Y]
             for j in range(c * group, (c + 1) * group):
                 for which in range(2):
                     send_rec[a, j, which] = slot(place(px, column(j), py), which)
+        for a, rd in enumerate(near_first):
             if a:
                 pltpu.make_async_remote_copy(
                     src_ref=send_rec.at[a, span],
@@ -506,6 +512,14 @@
     def hand_on(total, full, summed, at, full_in, summed_in, home, peer, sems):
         for b in range(BOX_DEV):
             full[at, b] = total[b]
+        pltpu.make_async_remote_copy(
+            src_ref=full.at[at],
+            dst_ref=full_in.at[home],
+            send_sem=sems.at[0],
+            recv_sem=sems.at[1],
+            device_id=(peer, fn),
+            device_id_type=MESH,
+        ).start()
         summed[at] = weighted(total)
         pltpu.make_async_remote_copy(
             src_ref=summed.at[at],
@@ -513,14 +527,6 @@
             send_sem=sems.at[2],
             recv_sem=sems.at[3],
             device_id=(peer, 1 - fn),
-            device_id_type=MESH,
-        ).start()
-        pltpu.make_async_remote_copy(
-            src_ref=full.at[at],
-            dst_ref=full_in.at[home],
-            send_sem=sems.at[0],
-            recv_sem=sems.at[1],
-            device_id=(peer, fn),
             device_id_type=MESH,
         ).start()
 
@@ -557,7 +563,7 @@
     def far_sums():
         wait_for(far_recv.at[: Z - 1], far_sem.at[1])
         for d, rd in enumerate(far_first):
-            px, py = lax.rem(x + rd // Y, X), lax.rem(y + rd % Y, Y)
+            px, py = across[rd // Y], along[rd % Y]
             owner = place(px, z, py)
             total = none
             for s in range(2):
@@ -576,7 +582,7 @@
 
     for c in range(per):
         near_sums(c)
-        if c == per // 2 - 1:
+        if c == 0:
             far_sums()
 
     result = z_send[Z - 1]

time: 52 us -> 51.9 us (level)
  no operation moved by 1% of the time
where the time goes in v4:
time: 51.9 us; the launch traced here: 51.7 us
  Pallas kernels  50.4 us (97%)
  between operations  1.29 us (2%)
    pallas_call x1, Pallas kernels, body(): pl.pallas_call(functools.partial(kernel, (X, Z, Y)), out_shape=(jax.Shape...  48.8 us
    pallas_call x1, Pallas kernels, body(): pl.pallas_call(hand_over, out_shape=(jax.ShapeDtypeStruct((BOX_DEV, funcs...  1.68 us

profile of v4, /device:TPU:1, one launch (start us, length us, event | category | flops | bytes accessed | tf_op | source)
XLA Modules:
  0.0 51.7 jit_solution(3923087887617204808)
XLA Ops:
  1.3 48.8 %shard_map.167 = (f32[4,8,128]{2,1,0:T(8,128)}, f32[4,128]{1,0:T(4,128)}) custom-call(f32[48,8,320]{2,1,0:T(8,128)} %rhs_hbm.1, bf16[48,320,320]{2,1,0:T(8,128)(2,1)} %dinv_hbm.1, f32[6,80,320]{2,1,0:T(8,128)} %bitcast.7, f32[6,80,320]{2,1,0:T(8,128)} %lift_hbm.1, f32[6,48]{1,0:T(8,128)} %bitcast.8, s32[6,48]{1,0:T(8,128)} %bitcast.9, s32[48]{0:T(128)} %colour_hbm.1, ...), custom_call_target="tpu_custom_call" | custom-call | tf_op jit(solution)/shard_map/pallas_call | solution.py:646
  50.1 1.7 %shard_map.168 = (f32[4,8,128]{2,1,0:T(8,128)}, f32[4,128]{1,0:T(4,128)}) custom-call(f32[4,8,128]{2,1,0:T(8,128)} %get-tuple-element.4.grad_in, f32[4,128]{1,0:T(4,128)} %get-tuple-element.5.combined_in), custom_call_target="tpu_custom_call" | custom-call | tf_op jit(solution)/shard_map/pallas_call | solution.py:735
